TPU v7x, 256 devices: a whole 4x4x8 slice. The times are simulated.
256 devices in a mesh: dp: 4 (over x), expert: 64 (over y, z, core).
Axes of the slice: x: 4, y: 4, z: 8, core: 2. Of those that a mesh axis runs over, the one named last changes fastest.
Arguments:
- saved_input: bfloat16 [8192, 2048], P(('dp', 'expert')), may hold values from -6 to 6
- output_grad: bfloat16 [8192, 2048], P(('dp', 'expert')), may hold values from -6 to 6
- route_probs: float32 [8192, 8], P(('dp', 'expert')), may hold values from 0.02 to 0.4
- expert_choice: int32 [8192, 8], P(('dp', 'expert')), may hold values from 0 to 127, all different within a row; in each aligned block of 32 rows (0 to 31, 32 to 63, ...) at most 3 rows name the same one
- slot_expert: int32 [4, 64], replicated, may hold values from 0 to 127, as said below
- frozen_gate: bfloat16 [256, 2048, 768], P(('dp', 'expert')), as said below
- frozen_up: bfloat16 [256, 2048, 768], P(('dp', 'expert')), as said below
- frozen_down: bfloat16 [256, 768, 2048], P(('dp', 'expert')), as said below
- adapter_in: float32 [128, 64, 768], P('expert', 'dp'), may hold values from -0.21875 to 0.21875
- adapter_out: float32 [128, 64, 2048], P('expert', 'dp'), may hold values from -0.125 to 0.125
- moment_in: float32 [128, 64, 768], P('expert', 'dp'), may hold values from -3 to 3
- moment_out: float32 [128, 64, 2048], P('expert', 'dp'), may hold values from -3 to 3
- second_in: float32 [128, 64, 768], P('expert', 'dp'), may hold values from 0.01 to 1
- second_out: float32 [128, 64, 2048], P('expert', 'dp'), may hold values from 0.01 to 1
Outputs:
- input_grad: bfloat16 [8192, 2048], P(('dp', 'expert'))
- step_in: float32 [128, 64, 768], P('expert', 'dp')
- step_out: float32 [128, 64, 2048], P('expert', 'dp')
- momentum_in: float32 [128, 64, 768], P('expert', 'dp')
- momentum_out: float32 [128, 64, 2048], P('expert', 'dp')
- variance_in: float32 [128, 64, 768], P('expert', 'dp')
- variance_out: float32 [128, 64, 2048], P('expert', 'dp')
- replica_in: bfloat16 [256, 64, 768], P(('dp', 'expert'))
- replica_out: bfloat16 [256, 64, 2048], P(('dp', 'expert'))
Inputs may be any that keep to these rules, and one draw needn't show every extreme that they name: `expert_choice`: among the rows of one device no expert is named more than 3 times. `slot_expert`: the slots of index j of the expert axis host only experts 2 * j to 2 * j + 1, and each of these at least once. `frozen_gate`: slots that host the same expert hold the same frozen weights. `frozen_up`: slots that host the same expert hold the same frozen weights. `frozen_down`: slots that host the same expert hold the same frozen weights.
All inputs are finite; a program needn't handle non-finite values.
Results may differ from a plain program's by a relative error of at most 0.012.
Values may be sent and summed in bfloat16 or wider, within the bound.
A program may use at most 128 MiB of HBM per device.

v0:
```python
import jax
import jax.numpy as jnp
from jax import lax
from jax.sharding import PartitionSpec as P

STEP = 100


adapter_scale_factor = 2.0
beta_one = 0.9
beta_two = 0.999
decay_rate = 0.01
adam_eps = 1e-08


def contract_product(left, right, left_dim, right_dim):
    return lax.dot_general(
        left, right, (((left_dim,), (right_dim,)), ((), ())), preferred_element_type=jnp.float32
    )


def route_rows(choice_flat, slot_expert, source, local_experts):
    column = choice_flat // local_experts
    hosted = (jnp.take(slot_expert, column, axis=1) == choice_flat[None, :]).astype(jnp.int32)
    counts = jnp.sum(hosted, axis=0)
    picked = source % counts
    running = jnp.cumsum(hosted, axis=0) - 1
    chosen = hosted * (running == picked[None, :]).astype(jnp.int32)
    dp_ids = jnp.arange(hosted.shape[0], dtype=jnp.int32)
    dest_row = jnp.sum(chosen * dp_ids[:, None], axis=0)
    row_ids = jnp.arange(choice_flat.shape[0], dtype=jnp.int32)
    earlier = (choice_flat[None, :] == choice_flat[:, None]) & (row_ids[None, :] < row_ids[:, None])
    rank = jnp.sum(earlier.astype(jnp.int32), axis=1)
    return (dest_row, column, rank)


def pack_rows(saved_input, scaled, position, buffer_size, top_count, shape_out):
    row_count = scaled.shape[0]
    row_ids = jnp.arange(row_count, dtype=jnp.int32)
    filler = jnp.full((buffer_size,), row_count, jnp.int32).at[position].set(row_ids)
    send_input = jnp.take(saved_input, filler // top_count, axis=0, mode="fill", fill_value=0)
    send_grad = jnp.take(scaled, filler, axis=0, mode="fill", fill_value=0)
    return (send_input.reshape(shape_out), send_grad.reshape(shape_out))


def adamw(param, grad, first, second):
    first_new = beta_one * first + (1.0 - beta_one) * grad
    second_new = beta_two * second + (1.0 - beta_two) * grad * grad
    corr_one = 1.0 - beta_one**STEP
    corr_two = 1.0 - beta_two**STEP
    step_dir = (
        first_new / corr_one / (jnp.sqrt(second_new / corr_two) + adam_eps) + decay_rate * param
    )
    return (step_dir, first_new, second_new)


def per_device(
    saved_input,
    output_grad,
    route_probs,
    expert_choice,
    slot_expert,
    frozen_gate,
    frozen_up,
    frozen_down,
    adapter_in,
    adapter_out,
    moment_in,
    moment_out,
    second_in,
    second_out,
):
    dp_count = lax.axis_size("dp")
    expert_count = lax.axis_size("expert")
    dp_index = lax.axis_index("dp")
    column_index = lax.axis_index("expert")
    local_experts = adapter_in.shape[0]
    token_count, top_count = expert_choice.shape
    width = saved_input.shape[1]
    row_count = token_count * top_count
    capacity = max(2, -(-3 * row_count // (2 * local_experts * expert_count)))
    buffer_size = dp_count * expert_count * capacity
    source = dp_index * expert_count + column_index
    choice_flat = expert_choice.reshape(row_count)
    dest_row, column, rank = route_rows(choice_flat, slot_expert, source, local_experts)
    scaled = (
        (route_probs[:, :, None] * output_grad[:, None, :].astype(jnp.float32))
        .astype(jnp.bfloat16)
        .reshape(row_count, width)
    )
    slot_shape = (dp_count, expert_count, capacity, width)
    position = (dest_row * expert_count + column) * capacity + rank
    send_input, send_grad = pack_rows(
        saved_input, scaled, position, buffer_size, top_count, slot_shape
    )
    arrived_input, arrived_grad = (
        lax.all_to_all(
            lax.all_to_all(send_input, "dp", split_axis=0, concat_axis=0, tiled=True),
            "expert",
            split_axis=1,
            concat_axis=1,
            tiled=True,
        ),
        lax.all_to_all(
            lax.all_to_all(send_grad, "dp", split_axis=0, concat_axis=0, tiled=True),
            "expert",
            split_axis=1,
            concat_axis=1,
            tiled=True,
        ),
    )
    fetched_in, fetched_out = (
        lax.all_gather(adapter_in.astype(jnp.bfloat16), "dp", axis=1, tiled=True),
        lax.all_gather(adapter_out.astype(jnp.bfloat16), "dp", axis=1, tiled=True),
    )
    hosted_local = slot_expert[dp_index, column_index] - local_experts * column_index
    owned_input = lax.dynamic_index_in_dim(fetched_in, hosted_local, 0, keepdims=False)
    own_out = lax.dynamic_index_in_dim(fetched_out, hosted_local, 0, keepdims=False)
    buffer_rows = arrived_input.reshape(buffer_size, width)
    gradient_row_block = arrived_grad.reshape(buffer_size, width)
    gate_weight = frozen_gate[0]
    up_weight = frozen_up[0]
    down_weight = frozen_down[0]
    gate_pre = jnp.dot(buffer_rows, gate_weight, preferred_element_type=jnp.float32)
    up_pre = jnp.dot(buffer_rows, up_weight, preferred_element_type=jnp.float32)
    sigmoid_gate = jax.nn.sigmoid(gate_pre)
    hidden_state = (gate_pre * sigmoid_gate * up_pre).astype(jnp.bfloat16)
    low_rank_input = contract_product(hidden_state, owned_input, 1, 1).astype(jnp.bfloat16)
    low_rank_gradient = contract_product(gradient_row_block, own_out, 1, 1).astype(jnp.bfloat16)
    hidden_gradient = contract_product(gradient_row_block, down_weight, 1, 1)
    hidden_gradient = hidden_gradient + adapter_scale_factor * jnp.dot(
        low_rank_gradient, owned_input, preferred_element_type=jnp.float32
    )
    up_grad = (hidden_gradient * gate_pre * sigmoid_gate).astype(jnp.bfloat16)
    gate_grad = (
        hidden_gradient * up_pre * sigmoid_gate * (1.0 + gate_pre * (1.0 - sigmoid_gate))
    ).astype(jnp.bfloat16)
    back_rows = (
        contract_product(gate_grad, gate_weight, 1, 1) + contract_product(up_grad, up_weight, 1, 1)
    ).astype(jnp.bfloat16)
    incoming_gradient = adapter_scale_factor * contract_product(
        low_rank_gradient, hidden_state, 0, 0
    )
    outgoing_gradient = adapter_scale_factor * contract_product(
        low_rank_input, gradient_row_block, 0, 0
    )
    back_block = back_rows.reshape(dp_count, expert_count, capacity, width)
    returned = lax.all_to_all(
        lax.all_to_all(back_block, "dp", split_axis=0, concat_axis=0, tiled=True),
        "expert",
        split_axis=1,
        concat_axis=1,
        tiled=True,
    )
    per_row = jnp.take(returned.reshape(buffer_size, width), position, axis=0)
    input_grad = jnp.sum(
        per_row.reshape(token_count, top_count, width).astype(jnp.float32), axis=1
    ).astype(jnp.bfloat16)
    selector = (jnp.arange(local_experts, dtype=jnp.int32) == hosted_local).astype(jnp.float32)
    placed_in = selector[:, None, None] * incoming_gradient[None, :, :]
    placed_out = selector[:, None, None] * outgoing_gradient[None, :, :]
    summed_in, summed_out = (
        lax.psum_scatter(placed_in, "dp", scatter_dimension=1, tiled=True),
        lax.psum_scatter(placed_out, "dp", scatter_dimension=1, tiled=True),
    )
    step_in, momentum_in, variance_in = adamw(adapter_in, summed_in, moment_in, second_in)
    step_out, momentum_out, variance_out = adamw(adapter_out, summed_out, moment_out, second_out)
    copied_in, copied_out = (
        lax.all_gather(step_in.astype(jnp.bfloat16), "dp", axis=1, tiled=True),
        lax.all_gather(step_out.astype(jnp.bfloat16), "dp", axis=1, tiled=True),
    )
    replica_in = lax.dynamic_index_in_dim(copied_in, hosted_local, 0, keepdims=True)
    replica_out = lax.dynamic_index_in_dim(copied_out, hosted_local, 0, keepdims=True)
    return (
        input_grad,
        step_in,
        step_out,
        momentum_in,
        momentum_out,
        variance_in,
        variance_out,
        replica_in,
        replica_out,
    )


def solution(mesh):
    return jax.shard_map(
        per_device,
        mesh=mesh,
        in_specs=(
            P(("dp", "expert"), None),
            P(("dp", "expert"), None),
            P(("dp", "expert"), None),
            P(("dp", "expert"), None),
            P(),
            P(("dp", "expert"), None, None),
            P(("dp", "expert"), None, None),
            P(("dp", "expert"), None, None),
            P("expert", "dp", None),
            P("expert", "dp", None),
            P("expert", "dp", None),
            P("expert", "dp", None),
            P("expert", "dp", None),
            P("expert", "dp", None),
        ),
        out_specs=(
            P(("dp", "expert"), None),
            P("expert", "dp", None),
            P("expert", "dp", None),
            P("expert", "dp", None),
            P("expert", "dp", None),
            P("expert", "dp", None),
            P("expert", "dp", None),
            P(("dp", "expert"), None, None),
            P(("dp", "expert"), None, None),
        ),
        check_vma=False,
    )
```

profile of v0, /device:TPU:1, one launch (start us, length us, event | category | flops | bytes accessed | tf_op | source)
XLA Modules:
  0.0 540.5 jit_solution(13556978153045774076)
XLA Ops:
  20.8 9.1 %gather.26 = bf16[4,64,3,2048]{3,2,1,0:T(4,128)(2,1)} reshape(bf16[768,2048]{1,0:T(8,128)(2,1)} %gather_fusion.2) | data formatting | bytes 6291456 | tf_op jit(solution)/shard_map/jit(_take)/gather | solution.py:41
  38.3 5.2 all-to-all-start.2
  46.0 8.5 %gather_fusion.1 = bf16[768,2048]{1,0:T(8,128)(2,1)} fusion(bf16[256,2048]{1,0:T(8,128)(2,1)} %fusion.9, s32[1024]{0:T(1024)S(1)} %pad_clamp_fusion.2), kind=kCustom, calls=%fused_computation.1 | custom fusion | bytes 6294528 | tf_op jit(solution)/shard_map/jit(_take)/gather | solution.py:42
  54.6 9.1 %gather.24 = bf16[4,64,3,2048]{3,2,1,0:T(4,128)(2,1)} reshape(bf16[768,2048]{1,0:T(8,128)(2,1)} %gather_fusion.1) | data formatting | bytes 6291456 | tf_op jit(solution)/shard_map/jit(_take)/gather | solution.py:42
  71.8 7.2 %all-to-all-done.2 = bf16[4,64,3,2048]{3,1,2,0:T(8,128)(2,1)} async-done(((bf16[4,64,3,2048]{3,1,2,0:T(8,128)(2,1)}), bf16[4,64,3,2048]{3,1,2,0:T(8,128)(2,1)}, u32[]{:S(2)}, u32[]{:S(2)}) %all-to-all-start.2) | async-done | bytes 3145760 | tf_op jit(solution)/shard_map/all_to_all | solution.py:98
  79.0 4.7 all-to-all-start
  83.6 6.1 %copy.62 = bf16[4,64,3,2048]{3,0,2,1:T(4,128)(2,1)} copy(bf16[4,64,3,2048]{3,1,2,0:T(8,128)(2,1)} %all-to-all-done.2) | data formatting | bytes 6291456 | tf_op jit(solution)/shard_map/all_to_all | solution.py:98
  89.7 28.1 %all-to-all-done = bf16[4,64,3,2048]{3,1,2,0:T(8,128)(2,1)} async-done(((bf16[4,64,3,2048]{3,1,2,0:T(8,128)(2,1)}), bf16[4,64,3,2048]{3,1,2,0:T(8,128)(2,1)}, u32[]{:S(2)}, u32[]{:S(2)}) %all-to-all-start) | async-done | bytes 3145760 | tf_op jit(solution)/shard_map/all_to_all | solution.py:105
  117.8 19.0 %all-to-all-start.3 = ((bf16[4,64,3,2048]{3,0,2,1:T(4,128)(2,1)}), bf16[4,64,3,2048]{3,0,2,1:T(4,128)(2,1)}, u32[]{:S(2)}, u32[]{:S(2)}) async-start(bf16[4,64,3,2048]{3,0,2,1:T(4,128)(2,1)} %copy.62), calls=%async_computation.3 | async-start | bytes 6291456 | tf_op jit(solution)/shard_map/all_to_all | solution.py:97
  136.8 6.0 %copy.59 = bf16[4,64,3,2048]{3,0,2,1:T(4,128)(2,1)} copy(bf16[4,64,3,2048]{3,1,2,0:T(8,128)(2,1)} %all-to-all-done) | data formatting | bytes 6291456 | tf_op jit(solution)/shard_map/all_to_all | solution.py:105
  142.8 67.2 %all-to-all-done.3 = bf16[4,64,3,2048]{3,0,2,1:T(4,128)(2,1)} async-done(((bf16[4,64,3,2048]{3,0,2,1:T(4,128)(2,1)}), bf16[4,64,3,2048]{3,0,2,1:T(4,128)(2,1)}, u32[]{:S(2)}, u32[]{:S(2)}) %all-to-all-start.3) | async-done | bytes 3145760 | tf_op jit(solution)/shard_map/all_to_all | solution.py:97
  210.1 6.3 %all-to-all-start.1 = ((bf16[4,64,3,2048]{3,0,2,1:T(4,128)(2,1)}), bf16[4,64,3,2048]{3,0,2,1:T(4,128)(2,1)}, u32[]{:S(2)}, u32[]{:S(2)}) async-start(bf16[4,64,3,2048]{3,0,2,1:T(4,128)(2,1)} %copy.59), calls=%async_computation.1 | async-start | bytes 6291456 | tf_op jit(solution)/shard_map/all_to_all | solution.py:104
  218.4 10.4 %all_gather.13 = bf16[2,64,768]{2,1,0:T(8,128)(2,1)S(1)} all-gather(bf16[2,16,768]{2,1,0:T(8,128)(2,1)S(1)} %convert_element_type.60), channel_id=1, replica_groups=mesh['dp'=4,'expert'=64] {'dp'}, dimensions={1}, use_global_device_ids=true | all-gather | bytes 245760 | tf_op jit(solution)/shard_map/all_gather | solution.py:113
  228.8 6.5 %copy.63 = bf16[4,64,3,2048]{3,2,1,0:T(4,128)(2,1)} copy(bf16[4,64,3,2048]{3,0,2,1:T(4,128)(2,1)} %all-to-all-done.3) | data formatting | bytes 6291456 | tf_op jit(solution)/shard_map/all_to_all | solution.py:97
  235.4 9.0 %reshape.237 = bf16[768,2048]{1,0:T(8,128)(2,1)} reshape(bf16[4,64,3,2048]{3,2,1,0:T(4,128)(2,1)} %copy.63) | data formatting | bytes 6291456 | tf_op jit(solution)/shard_map/reshape | solution.py:119
  244.3 45.5 %all-to-all-done.1 = bf16[4,64,3,2048]{3,0,2,1:T(4,128)(2,1)} async-done(((bf16[4,64,3,2048]{3,0,2,1:T(4,128)(2,1)}), bf16[4,64,3,2048]{3,0,2,1:T(4,128)(2,1)}, u32[]{:S(2)}, u32[]{:S(2)}) %all-to-all-start.1) | async-done | bytes 3145760 | tf_op jit(solution)/shard_map/all_to_all | solution.py:104
  289.8 6.5 %copy.60 = bf16[4,64,3,2048]{3,2,1,0:T(4,128)(2,1)} copy(bf16[4,64,3,2048]{3,0,2,1:T(4,128)(2,1)} %all-to-all-done.1) | data formatting | bytes 6291456 | tf_op jit(solution)/shard_map/all_to_all | solution.py:104
  296.3 8.8 %reshape.236 = bf16[768,2048]{1,0:T(8,128)(2,1)} reshape(bf16[4,64,3,2048]{3,2,1,0:T(4,128)(2,1)} %copy.60) | data formatting | bytes 6291456 | tf_op jit(solution)/shard_map/reshape | solution.py:120
  305.1 5.6 %fusion.2 = f32[768,768]{1,0:T(8,128)S(1)} fusion(bf16[768,2048]{1,0:T(8,128)(2,1)} %reshape.237, bf16[1,2048,768]{2,1,0:T(8,128)(2,1)} %param.19), kind=kOutput, calls=%fused_computation.10 | convolution fusion | flops 2415919104 | bytes 8650752 | tf_op jit(solution)/shard_map/dot_general | solution.py:124
  321.8 6.9 %fusion.7 = f32[768,768]{1,0:T(8,128)} fusion(bf16[768,2048]{1,0:T(8,128)(2,1)} %reshape.236, bf16[1,768,2048]{2,1,0:T(8,128)(2,1)} %param.21), kind=kOutput, calls=%fused_computation.15 | convolution fusion | flops 2415919104 | bytes 8650752 | tf_op jit(solution)/shard_map/dot_general | solution.py:17
  328.6 12.9 %reduce-scatter.5.cloned.1.call-done = f32[2,16,2048]{2,1,0:T(8,128)} async-done(((f32[2,64,2048]{2,1,0:T(8,128)}), f32[2,16,2048]{2,1,0:T(8,128)}) %reduce-scatter.5.cloned.1.call-update) | async-done | bytes 262160 | tf_op jit(solution)/shard_map/reduce_scatter | solution.py:164
  343.9 11.2 %all_gather.12 = bf16[2,64,2048]{2,1,0:T(8,128)(2,1)S(1)} all-gather(bf16[2,16,2048]{2,1,0:T(8,128)(2,1)S(1)} %get-tuple-element.23), channel_id=1, replica_groups=mesh['dp'=4,'expert'=64] {'dp'}, dimensions={1}, use_global_device_ids=true | all-gather | bytes 655360 | tf_op jit(solution)/shard_map/all_gather | solution.py:114
  367.5 9.1 %reshape.238 = bf16[4,64,3,2048]{3,2,1,0:T(4,128)(2,1)} reshape(bf16[768,2048]{1,0:T(8,128)(2,1)} %add_convert_fusion) | data formatting | bytes 6291456 | tf_op jit(solution)/shard_map/reshape | solution.py:147
  381.1 36.2 %all_to_all.30 = bf16[4,64,3,2048]{3,1,2,0:T(8,128)(2,1)S(1)} all-to-all(bf16[4,64,3,2048]{3,1,2,0:T(8,128)(2,1)S(1)} %copy.64), channel_id=1, replica_groups=mesh['dp'=4,'expert'=64] {'dp'}, dimensions={0} | all-to-all | bytes 6291456 | tf_op jit(solution)/shard_map/all_to_all | solution.py:149
  421.4 15.0 %all-to-all-start.5 = ((bf16[4,64,3,2048]{3,0,2,1:T(4,128)(2,1)}), bf16[4,64,3,2048]{3,0,2,1:T(4,128)(2,1)}, u32[]{:S(2)}, u32[]{:S(2)}) async-start(bf16[4,64,3,2048]{3,0,2,1:T(4,128)(2,1)} %copy.65), calls=%async_computation.5 | async-start | bytes 6291456 | tf_op jit(solution)/shard_map/all_to_all | solution.py:148
  439.1 11.1 %all_gather.15 = bf16[2,64,2048]{2,1,0:T(8,128)(2,1)S(1)} all-gather(bf16[2,16,2048]{2,1,0:T(8,128)(2,1)S(1)} %copy-done.4), channel_id=1, replica_groups=mesh['dp'=4,'expert'=64] {'dp'}, dimensions={1}, use_global_device_ids=true | all-gather | bytes 655360 | tf_op jit(solution)/shard_map/all_gather | solution.py:170
  451.0 10.1 %reduce-scatter.3.cloned.1.call-done = f32[2,16,768]{2,1,0:T(8,128)} async-done(((f32[2,64,768]{2,1,0:T(8,128)}), f32[2,16,768]{2,1,0:T(8,128)}) %reduce-scatter.3.cloned.1.call-update) | async-done | bytes 98320 | tf_op jit(solution)/shard_map/reduce_scatter | solution.py:163
  462.8 10.7 %all_gather.14 = bf16[2,64,768]{2,1,0:T(8,128)(2,1)S(1)} all-gather(bf16[2,16,768]{2,1,0:T(8,128)(2,1)S(1)} %get-tuple-element.13), channel_id=1, replica_groups=mesh['dp'=4,'expert'=64] {'dp'}, dimensions={1}, use_global_device_ids=true | all-gather | bytes 245760 | tf_op jit(solution)/shard_map/all_gather | solution.py:169
  474.1 35.7 %all-to-all-done.5 = bf16[4,64,3,2048]{3,0,2,1:T(4,128)(2,1)} async-done(((bf16[4,64,3,2048]{3,0,2,1:T(4,128)(2,1)}), bf16[4,64,3,2048]{3,0,2,1:T(4,128)(2,1)}, u32[]{:S(2)}, u32[]{:S(2)}) %all-to-all-start.5) | async-done | bytes 3145760 | tf_op jit(solution)/shard_map/all_to_all | solution.py:148
  509.8 6.5 %copy.66 = bf16[4,64,3,2048]{3,2,1,0:T(4,128)(2,1)} copy(bf16[4,64,3,2048]{3,0,2,1:T(4,128)(2,1)} %all-to-all-done.5) | data formatting | bytes 6291456 | tf_op jit(solution)/shard_map/all_to_all | solution.py:148
  516.3 8.8 %reshape.239 = bf16[768,2048]{1,0:T(8,128)(2,1)} reshape(bf16[4,64,3,2048]{3,2,1,0:T(4,128)(2,1)} %copy.66) | data formatting | bytes 6291456 | tf_op jit(solution)/shard_map/reshape | solution.py:155
  525.1 5.6 %gather_fusion.3 = bf16[256,2048]{1,0:T(8,128)(2,1)} fusion(bf16[768,2048]{1,0:T(8,128)(2,1)} %reshape.239, s32[1024]{0:T(1024)S(1)} %pad_clamp_fusion), kind=kCustom, calls=%fused_computation.3 | custom fusion | bytes 2098176 | tf_op jit(solution)/shard_map/jit(_take)/gather | solution.py:155
  (98 shorter events, 76.5 us)
Async XLA Ops:
  7.2 303.6 %copy-start = (bf16[1,2048,768]{2,1,0:T(8,128)(2,1)S(1)}, bf16[1,2048,768]{2,1,0:T(8,128)(2,1)}, u32[]{:S(2)}) copy-start(bf16[1,2048,768]{2,1,0:T(8,128)(2,1)} %param.20) | copy-start | bytes 9437188
  7.2 9.4 %copy-start.1 = (bf16[32,2048]{1,0:T(8,128)(2,1)S(1)}, bf16[32,2048]{1,0:T(8,128)(2,1)}, u32[]{:S(2)}) copy-start(bf16[32,2048]{1,0:T(8,128)(2,1)} %param.14) | copy-start | bytes 393220
  11.4 0.6 copy-start.6
  13.9 7.0 %copy-start.8 = (s32[256]{0:T(256)}, s32[256]{0:T(256)S(1)}, u32[]{:S(2)}) copy-start(s32[256]{0:T(256)S(1)} %broadcast_multiply_fusion.2) | copy-start | bytes 3076
  14.6 0.6 copy-start.11
  38.3 6.4 %copy-start.10 = (f32[32,8]{0,1:T(8,128)S(1)}, f32[32,8]{0,1:T(8,128)}, u32[]{:S(2)}) copy-start(f32[32,8]{0,1:T(8,128)} %param.16) | copy-start | bytes 3076
  38.3 40.7 %all-to-all-start.2 = ((bf16[4,64,3,2048]{3,1,2,0:T(8,128)(2,1)}), bf16[4,64,3,2048]{3,1,2,0:T(8,128)(2,1)}, u32[]{:S(2)}, u32[]{:S(2)}) async-start(bf16[4,64,3,2048]{3,1,2,0:T(8,128)(2,1)} %copy.61), calls=%async_computation.2 | async-start | bytes 6291456 | tf_op jit(solution)/shard_map/all_to_all | solution.py:98
  79.0 38.8 %all-to-all-start = ((bf16[4,64,3,2048]{3,1,2,0:T(8,128)(2,1)}), bf16[4,64,3,2048]{3,1,2,0:T(8,128)(2,1)}, u32[]{:S(2)}, u32[]{:S(2)}) async-start(bf16[4,64,3,2048]{3,1,2,0:T(8,128)(2,1)} %copy.58), calls=%async_computation | async-start | bytes 6291456 | tf_op jit(solution)/shard_map/all_to_all | solution.py:105
  117.8 92.3 %all-to-all-start.3 = ((bf16[4,64,3,2048]{3,0,2,1:T(4,128)(2,1)}), bf16[4,64,3,2048]{3,0,2,1:T(4,128)(2,1)}, u32[]{:S(2)}, u32[]{:S(2)}) async-start(bf16[4,64,3,2048]{3,0,2,1:T(4,128)(2,1)} %copy.62), calls=%async_computation.3 | async-start | bytes 6291456 | tf_op jit(solution)/shard_map/all_to_all | solution.py:97
  142.8 75.5 %copy-start.5 = (f32[2,16,768]{2,1,0:T(8,128)S(1)}, f32[2,16,768]{2,1,0:T(8,128)}, u32[]{:S(2)}) copy-start(f32[2,16,768]{2,1,0:T(8,128)} %param.22) | copy-start | bytes 294916
  210.1 79.7 %all-to-all-start.1 = ((bf16[4,64,3,2048]{3,0,2,1:T(4,128)(2,1)}), bf16[4,64,3,2048]{3,0,2,1:T(4,128)(2,1)}, u32[]{:S(2)}, u32[]{:S(2)}) async-start(bf16[4,64,3,2048]{3,0,2,1:T(4,128)(2,1)} %copy.59), calls=%async_computation.1 | async-start | bytes 6291456 | tf_op jit(solution)/shard_map/all_to_all | solution.py:104
  216.4 125.2 %reduce-scatter.5.cloned.1.call-start = ((), (), s32[]{:S(2)}) async-start(), calls=%async_computation.9 | async-start | bytes 1310720 | tf_op jit(solution)/shard_map/reduce_scatter | solution.py:164
  228.8 90.7 %copy-start.13 = (f32[2]{0:T(128)}, f32[2]{0:T(128)S(1)}, u32[]{:S(2)}) copy-start(f32[2]{0:T(128)S(1)} %compare_convert_fusion) | copy-start | bytes 28
  305.1 5.6 %copy-start.2 = (bf16[768,2048]{1,0:T(8,128)(2,1)S(1)}, bf16[768,2048]{1,0:T(8,128)(2,1)}, u32[]{:S(2)}) copy-start(bf16[768,2048]{1,0:T(8,128)(2,1)} %reshape.237) | copy-start | bytes 9437188
  310.8 4.5 copy-start.16
  343.9 14.3 %copy-start.3 = (f32[768,768]{1,0:T(8,128)S(1)}, f32[768,768]{1,0:T(8,128)}, u32[]{:S(2)}) copy-start(f32[768,768]{1,0:T(8,128)} %fusion.7) | copy-start | bytes 7077892
  355.1 3.6 copy-start.17
  355.1 3.6 copy-start.18
  358.2 1.9 copy-start.15
  421.4 16.6 %copy-start.14 = (f32[2]{0:T(128)S(1)}, f32[2]{0:T(128)}, u32[]{:S(2)}) copy-start(f32[2]{0:T(128)} %copy-done.13) | copy-start | bytes 28
  421.4 17.5 %copy-start.9 = (s32[256]{0:T(256)S(1)}, s32[256]{0:T(256)}, u32[]{:S(2)}) copy-start(s32[256]{0:T(256)} %copy-done.8) | copy-start | bytes 3076
  421.4 17.6 %copy-start.7 = (s32[256]{0:T(256)S(1)}, s32[256]{0:T(256)}, u32[]{:S(2)}) copy-start(s32[256]{0:T(256)} %convert_reduce_fusion) | copy-start | bytes 3076
  421.4 17.7 %copy-start.12 = (s32[256,1]{0,1:T(1,128)S(1)}, s32[256,1]{0,1:T(1,128)}, u32[]{:S(2)}) copy-start(s32[256,1]{0,1:T(1,128)} %copy-done.11) | copy-start | bytes 3076
  421.4 17.8 %copy-start.4 = (bf16[2,16,2048]{2,1,0:T(8,128)(2,1)S(1)}, bf16[2,16,2048]{2,1,0:T(8,128)(2,1)}, u32[]{:S(2)}) copy-start(bf16[2,16,2048]{2,1,0:T(8,128)(2,1)} %get-tuple-element.9) | copy-start | bytes 393220
  421.4 88.4 %all-to-all-start.5 = ((bf16[4,64,3,2048]{3,0,2,1:T(4,128)(2,1)}), bf16[4,64,3,2048]{3,0,2,1:T(4,128)(2,1)}, u32[]{:S(2)}, u32[]{:S(2)}) async-start(bf16[4,64,3,2048]{3,0,2,1:T(4,128)(2,1)} %copy.65), calls=%async_computation.5 | async-start | bytes 6291456 | tf_op jit(solution)/shard_map/all_to_all | solution.py:148
  436.3 24.7 %reduce-scatter.3.cloned.1.call-start = ((), (), s32[]{:S(2)}) async-start(), calls=%async_computation.8 | async-start | bytes 491520 | tf_op jit(solution)/shard_map/reduce_scatter | solution.py:163
Sparse Core Ops, SparseCore 0:
  321.9 19.6 reduce-scatter.4
  439.9 21.1 reduce-scatter.2
where the time goes:
time: 549 us; the launch traced here: 540 us
  waiting for transfers between devices  207 us (38%)
  local copies, waits for them, and re-layouts  131 us (24%)
  blocking collectives  79.6 us (14%)
  starting transfers between devices  50.2 us (9%)
  matrix products  33.8 us (6%)
  other arithmetic  24 us (4%)
  between operations  15.5 us (3%)
    all_to_all x1, waiting for transfers between devices, per_device(): lax.all_to_all(lax.all_to_all(send_input, 'dp', split_axis=0, concat_axis...  67.2 us
    all_to_all x1, waiting for transfers between devices, per_device(): lax.all_to_all(lax.all_to_all(send_grad, 'dp', split_axis=0, concat_axis=...  45.5 us
    all_to_all x1, blocking collectives, per_device(): lax.all_to_all(back_block, 'dp', split_axis=0, concat_axis=0, tiled=True)  36.2 us
    all_to_all x1, waiting for transfers between devices, per_device(): lax.all_to_all(lax.all_to_all(back_block, 'dp', split_axis=0, concat_axis...  35.7 us
    all_to_all x1, waiting for transfers between devices, per_device(): lax.all_to_all(send_grad, 'dp', split_axis=0, concat_axis=0, tiled=True)  28.1 us
    dot_general x6, matrix products, contract_product(): lax.dot_general(left, right, (((left_dim,), (right_dim,)), ((), ())), pre...  23.2 us
    all_to_all x1, starting transfers between devices, per_device(): lax.all_to_all(lax.all_to_all(send_input, 'dp', split_axis=0, concat_axis...  19 us
    gather x2, local copies, waits for them, and re-layouts, pack_rows(): send_grad = jnp.take(scaled, filler, axis=0, mode='fill', fill_value=0)  17.6 us
  transfers between devices with their start and end apart: 7, of which 7 were waited for; matrix products, arithmetic and copies ran while one was open for 13% of the time, Pallas kernels for 0%

commit v1 on v0

v1 whole, which is shorter than its diff:
```python
import functools

import jax
import jax.numpy as jnp
from jax import lax
from jax.experimental import pallas as pl
from jax.experimental.pallas import tpu as pltpu
from jax.sharding import PartitionSpec as P

MESH = pl.DeviceIdType.MESH
STEP = 100
SCALE = 2.0
BETA1 = 0.9
BETA2 = 0.999
DECAY = 0.01
EPS = 1e-08
ND, NY, NZ = 4, 4, 8
CAP = 3
NS = 2 * NZ
ROWS = CAP * NS
PLANE = NY * ROWS
ALL_ROWS = ND * PLANE
HALF = NZ // 2
NC = 4
BF = jnp.bfloat16
F32 = jnp.float32


def dot(a, b, dims=((1,), (0,))):
    return lax.dot_general(a, b, (dims, ((), ())), preferred_element_type=F32)


def choose(flag, a, b):
    return jnp.where(jnp.full(a.shape, flag, F32) > 0.5, a, b)


def adamw(param, grad, first, second):
    first_new = BETA1 * first + (1.0 - BETA1) * grad
    second_new = BETA2 * second + (1.0 - BETA2) * grad * grad
    corr_one = 1.0 - BETA1**STEP
    corr_two = 1.0 - BETA2**STEP
    step = first_new / corr_one / (jnp.sqrt(second_new / corr_two) + EPS) + DECAY * param
    return step, first_new, second_new


def kernel(
    x_ref, g_ref, meta_ref, slots_ref, wg_hbm, wu_hbm, wd_hbm, *rest
):
    adam_hbm, rest = rest[:6], rest[6:]
    (ig_out, st_in, st_out, mo_in, mo_out, va_in, va_out, re_in, re_out), rest = rest[:9], rest[9:]
    (
        wg, wu, wd, adam_in, adam_out, stage, zbuf, mbuf, pick, pick_t, weight, sendbuf, obuf, xbuf,
        gacc, uacc, hacc, lacc, hid, ugr, ggr, lgr, lin,
        bbuf, r1buf, r2buf, osum, rbuf, tok, zs1, zr1, zsn, zrn, fin, ig,
        ad_in, ad_out, cin, cout, gs_in, gs_out, gr_in, gr_out, ss_in, ss_out, rin, rout,
        hbm_sem, sib_s, sib_r, z_s, z_r, y_s, y_r, yl_s, x_s, x_r, a_s, a_r,
        b1_s, b1_r, b2_s, b2_r, q_s, q_r, ql_s, t_s, t_r, f_s, f_r, g_s, g_r, s_s, s_r,
    ) = rest
    D, H = wg.shape
    T = x_ref.shape[0]
    R = cin.shape[0] * cin.shape[1]
    CC = D // NC
    CH = CC // 2
    d = lax.axis_index("dp")
    j = lax.axis_index("expert")
    y = lax.div(j, 2 * NZ)
    z = lax.rem(lax.div(j, 2), NZ)
    k = lax.rem(j, 2)
    ok = 1 - k

    def col(yy, zz, kk):
        return (yy * NZ + zz) * 2 + kk

    def ymod(o):
        return lax.rem(y + o + NY, NY)

    def zmod(o):
        return lax.rem(z + o + NZ, NZ)

    def xmod(o):
        return lax.rem(d + o + ND, ND)

    sibling = (d, col(y, z, ok))
    up_z, down_z = (d, col(y, zmod(1), k)), (d, col(y, zmod(-1), k))
    right, left = (xmod(1), j), (xmod(-1), j)

    sent = []

    def send(src, dst, ss, rs, dev):
        c = pltpu.make_async_remote_copy(
            src_ref=src, dst_ref=dst, send_sem=ss, recv_sem=rs, device_id=dev, device_id_type=MESH
        )
        c.start()
        sent.append(c)

    def landed(dst, rs):
        pltpu.make_async_remote_copy(
            src_ref=dst, dst_ref=dst, send_sem=rs, recv_sem=rs, device_id=sibling, device_id_type=MESH
        ).wait_recv()

    loads = [
        pltpu.make_async_copy(wg_hbm.at[0], wg, hbm_sem.at[0]),
        pltpu.make_async_copy(wu_hbm.at[0], wu, hbm_sem.at[1]),
        pltpu.make_async_copy(wd_hbm.at[0], wd, hbm_sem.at[2]),
    ]
    adam_loads = []
    for i in range(3):
        adam_loads.append(pltpu.make_async_copy(adam_hbm[2 * i], adam_in.at[i], hbm_sem.at[3 + 2 * i]))
        adam_loads.append(pltpu.make_async_copy(adam_hbm[2 * i + 1], adam_out.at[i], hbm_sem.at[4 + 2 * i]))
    for c in adam_loads + loads:
        c.start()

    partners = [sibling, up_z, down_z]
    partners += [(d, col(ymod(o), z, kk)) for o in range(1, NY) for kk in range(2)]
    partners += [(xmod(o), j) for o in range(1, ND)]
    barrier = pltpu.get_barrier_semaphore()
    for dev in partners:
        pl.semaphore_signal(barrier, inc=1, device_id=dev, device_id_type=MESH)

    @pl.when(k == 0)
    def _():
        for c in range(NC):
            zbuf[c, z, 0] = x_ref[:, c * CC : (c + 1) * CC]
            stage[c] = g_ref[:, c * CC : (c + 1) * CC]

    @pl.when(k == 1)
    def _():
        for c in range(NC):
            zbuf[c, z, 1] = g_ref[:, c * CC : (c + 1) * CC]
            stage[c] = x_ref[:, c * CC : (c + 1) * CC]

    mbuf[z, k] = meta_ref[...]
    pl.semaphore_wait(barrier, len(partners))

    send(meta_ref, mbuf.at[z, k], sib_s.at[NC], sib_r.at[NC], sibling)
    for c in range(NC):
        send(stage.at[c], zbuf.at[c, z, k], sib_s.at[c], sib_r.at[c], sibling)

    def zref(c):
        return mbuf if c == NC else zbuf.at[c]

    def z_send(c, i):
        buf = zref(c)
        a, b = zmod(1 - i), zmod(i - 1)
        if i < HALF:
            send(buf.at[a], buf.at[a], z_s.at[c, 0, i - 1], z_r.at[c, 0, i - 1], up_z)
            send(buf.at[b], buf.at[b], z_s.at[c, 1, i - 1], z_r.at[c, 1, i - 1], down_z)
        else:
            send(buf.at[a, 0], buf.at[a, 0], z_s.at[c, 0, i - 1], z_r.at[c, 0, i - 1], up_z)
            send(buf.at[b, 1], buf.at[b, 1], z_s.at[c, 1, i - 1], z_r.at[c, 1, i - 1], down_z)

    def z_wait(c, i):
        buf = zref(c)
        a, b = zmod(-i), zmod(i)
        if i < HALF:
            landed(buf.at[a], z_r.at[c, 0, i - 1])
            landed(buf.at[b], z_r.at[c, 1, i - 1])
        else:
            landed(buf.at[a, 0], z_r.at[c, 0, i - 1])
            landed(buf.at[b, 1], z_r.at[c, 1, i - 1])

    def z_step(c, i):
        if i == 0:
            landed(zref(c).at[z, ok], sib_r.at[c])
        else:
            z_wait(c, i)
        if i < HALF:
            z_send(c, i + 1)

    def slot(q, jj):
        return slots_ref[q, jj].astype(F32)

    hosted = slot(d, j)
    first = (2 * j).astype(F32)
    both = (4 * j + 1).astype(F32)

    taken = jnp.float32(1.0)
    for q in range(ND):
        same = jnp.where(slot(q, j) == hosted, 1.0, 0.0)
        taken = taken * jnp.where(q < d, 1.0 - same, 1.0)
    mine = [jnp.float32(1.0)] + [
        taken * jnp.where(both - slot(xmod(-o), j) == hosted, 1.0, 0.0) for o in range(1, ND)
    ]

    def build_pick():
        groups = [
            mbuf[2 * q, 0] + mbuf[2 * q, 1] + mbuf[2 * q + 1, 0] + mbuf[2 * q + 1, 1]
            for q in range(NZ // 2)
        ]
        meta = jnp.concatenate(groups, axis=1)
        width = meta.shape[1]
        row = lax.broadcasted_iota(jnp.int32, (NS, width), 0)
        lane = lax.broadcasted_iota(jnp.int32, (NS, width), 1)
        experts = jnp.zeros((NS, width), F32)
        for o in range(NY):
            for kk in range(2):
                jj = col(ymod(o), z, kk)
                host = slot(d, jj)
                other = (4 * jj + 1).astype(F32) - host
                e = (o * 2 + kk) * 2
                experts = jnp.where(row == e, jnp.full((NS, width), host, F32), experts)
                experts = jnp.where(row == e + 1, jnp.full((NS, width), other, F32), experts)
        hit = jnp.zeros((NS, width), F32)
        prob = jnp.zeros((NS, width), F32)
        for kk in range(8):
            m = jnp.broadcast_to(meta[kk : kk + 1], (NS, width)) == experts
            hit = jnp.where(m, 1.0, hit)
            prob = jnp.where(m, jnp.broadcast_to(meta[8 + kk : 9 + kk], (NS, width)), prob)
        seg = lax.shift_right_logical(lane, 5) == row
        sa = lax.broadcasted_iota(jnp.int32, (width, width), 0)
        sb = lax.broadcasted_iota(jnp.int32, (width, width), 1)
        before = (sa < sb) & (lax.shift_right_logical(sa, 5) == lax.shift_right_logical(sb, 5))
        rank = dot(hit.astype(BF), jnp.where(before, 1.0, 0.0).astype(BF))
        key = jnp.where(hit > 0.5, rank, -1.0)
        unit = jnp.where(k == 0, 1.0, 0.0)
        for e in range(4 * NY):
            for r in range(CAP):
                at = (e * CAP + r) * NS
                m = (jnp.broadcast_to(key[e : e + 1], (NS, width)) == float(r)) & seg
                block = jnp.where(m, 1.0, 0.0)
                pick[pl.ds(at, NS), :] = block.astype(BF)
                total = jnp.sum(block * jnp.broadcast_to(prob[e : e + 1], (NS, width)), axis=1, keepdims=True)
                total = unit + (1.0 - unit) * total
                weight[pl.ds(at, NS), :] = jnp.broadcast_to(total, (NS, weight.shape[1]))

    def select(c):
        tokens = zbuf[c].reshape(NS * T, CC)
        for o in (2, 1, 3, 0):
            for kk in range(2):
                t = o * 2 + kk
                rows = pl.ds(t * 2 * ROWS, 2 * ROWS)
                got = dot(pick[rows, :], tokens)
                w = weight[rows, :]
                got = jnp.concatenate([got[:, i : i + 128] * w for i in range(0, CC, 128)], axis=1)
                sendbuf[c, t] = got.astype(BF).reshape(2, ROWS, CC)
                if o:
                    dev = (d, col(ymod(o), z, kk))
                    send(sendbuf.at[c, t, 0], xbuf.at[c, k, 0, o], y_s.at[c, t, 0], y_r.at[c, o, k, 0], dev)
                    send(sendbuf.at[c, t, 1], obuf.at[c, k, o], y_s.at[c, t, 1], y_r.at[c, o, k, 1], dev)
        send(sendbuf.at[c, ok, 0], xbuf.at[c, k, 0, 0], y_s.at[c, 0, 0], y_r.at[c, 0, k, 0], sibling)
        send(sendbuf.at[c, ok, 1], obuf.at[c, k, 0], y_s.at[c, 0, 1], y_r.at[c, 0, k, 1], sibling)
        own = [
            pltpu.make_async_copy(sendbuf.at[c, k, 0], xbuf.at[c, k, 0, 0], yl_s.at[c, 0]),
            pltpu.make_async_copy(sendbuf.at[c, k, 1], obuf.at[c, k, 0], yl_s.at[c, 1]),
        ]
        for copy in own:
            copy.start()
        return own

    def y_wait(c, own):
        for o in range(1, NY):
            for kk in range(2):
                landed(obuf.at[c, kk, o], y_r.at[c, o, kk, 1])
        landed(obuf.at[c, ok, 0], y_r.at[c, 0, ok, 1])
        own[1].wait()
        send(obuf.at[c], xbuf.at[c, :, 1], x_s.at[c, 0], x_r.at[c, 0], right)
        send(obuf.at[c], xbuf.at[c, :, 3], x_s.at[c, 1], x_r.at[c, 1], left)
        for o in range(1, NY):
            for kk in range(2):
                landed(xbuf.at[c, kk, 0, o], y_r.at[c, o, kk, 0])
        landed(xbuf.at[c, ok, 0, 0], y_r.at[c, 0, ok, 0])
        own[0].wait()

    def x_forward(c):
        landed(xbuf.at[c, :, 1], x_r.at[c, 0])
        landed(xbuf.at[c, :, 3], x_r.at[c, 1])
        send(xbuf.at[c, 0, 1], xbuf.at[c, 0, 2], x_s.at[c, 2], x_r.at[c, 2], right)
        send(xbuf.at[c, 1, 3], xbuf.at[c, 1, 2], x_s.at[c, 3], x_r.at[c, 3], left)

    def x_wait(c):
        landed(xbuf.at[c, 0, 2], x_r.at[c, 2])
        landed(xbuf.at[c, 1, 2], x_r.at[c, 3])

    NB = 256

    def accumulate(c):
        def add(acc, cols, value):
            n = value.shape[1]
            for p in range(ND):
                rows = slice(p * PLANE, (p + 1) * PLANE)
                part = value[rows]
                if p:
                    part = choose(mine[p], part, jnp.zeros((PLANE, n), F32))
                if c == 0:
                    acc[rows, cols] = part
                else:
                    acc[rows, cols] += part

        def body(n, carry):
            cols = pl.ds(pl.multiple_of(n * NB, NB), NB)
            rows_x = xbuf[c, 0].reshape(ALL_ROWS, CC)
            add(gacc, cols, dot(rows_x, wg[c * CC : (c + 1) * CC, cols]))
            add(uacc, cols, dot(rows_x, wu[c * CC : (c + 1) * CC, cols]))
            rows_g = xbuf[c, 1].reshape(ALL_ROWS, CC)
            add(hacc, cols, dot(rows_g, wd[cols, c * CC : (c + 1) * CC], ((1,), (1,))))
            return carry

        lax.fori_loop(0, H // NB, body, 0)
        rows_g = xbuf[c, 1].reshape(ALL_ROWS, CC)
        co = cout[:, :, c * CC : (c + 1) * CC].reshape(R, CC)
        add(lacc, slice(0, R), dot(rows_g, co, ((1,), (1,))))

    EB = 96

    def middle():
        ci = cin[...].reshape(R, H)

        def body(n, carry):
            rows = pl.ds(pl.multiple_of(n * EB, EB), EB)
            low = lacc[rows, :].astype(BF)
            lgr[rows, :] = low
            gate, up = gacc[rows, :], uacc[rows, :]
            hg = hacc[rows, :] + SCALE * dot(low, ci)
            sg = jax.nn.sigmoid(gate)
            act = gate * sg
            hidden = (act * up).astype(BF)
            hid[rows, :] = hidden
            ugr[rows, :] = (hg * act).astype(BF)
            ggr[rows, :] = (hg * up * sg * (1.0 + gate * (1.0 - sg))).astype(BF)
            lin[rows, :] = dot(hidden, ci, ((1,), (1,))).astype(BF)
            return carry

        lax.fori_loop(0, ALL_ROWS // EB, body, 0)

    def back(c):
        for h in range(2):
            lo = c * CC + h * CH
            r = dot(ggr[...], wg[lo : lo + CH, :], ((1,), (1,))) + dot(ugr[...], wu[lo : lo + CH, :], ((1,), (1,)))
            r = r.astype(BF).reshape(ND, NY, ROWS, CH)
            for p in range(ND):
                bbuf[c, p, h] = r[p]
        send(bbuf.at[c, 2, 0], r1buf.at[c, 0], b1_s.at[c, 0], b1_r.at[c, 0], right)
        send(bbuf.at[c, 2, 1], r1buf.at[c, 1], b1_s.at[c, 1], b1_r.at[c, 1], left)

    def back_forward(c):
        landed(r1buf.at[c, 0], b1_r.at[c, 0])
        bbuf[c, 3, 0] = bbuf[c, 3, 0] + r1buf[c, 0]
        send(bbuf.at[c, 3], r2buf.at[c, 0], b2_s.at[c, 0], b2_r.at[c, 0], right)
        landed(r1buf.at[c, 1], b1_r.at[c, 1])
        bbuf[c, 1, 1] = bbuf[c, 1, 1] + r1buf[c, 1]
        send(bbuf.at[c, 1], r2buf.at[c, 1], b2_s.at[c, 1], b2_r.at[c, 1], left)

    def y_back(c):
        for o in (2, 1, 3):
            for h in range(2):
                dev = (d, col(ymod(-o), z, h))
                send(bbuf.at[c, 0, h, o], rbuf.at[c, o * 2 + k, 0], q_s.at[c, o, h, 0], q_r.at[c, o, k, 0], dev)
        send(bbuf.at[c, 0, ok, 0], rbuf.at[c, k, 0], q_s.at[c, 0, 0, 0], q_r.at[c, 0, k, 0], sibling)
        own = [pltpu.make_async_copy(bbuf.at[c, 0, k, 0], rbuf.at[c, k, 0], ql_s.at[c, 0])]
        own[0].start()
        landed(r2buf.at[c, 0], b2_r.at[c, 0])
        landed(r2buf.at[c, 1], b2_r.at[c, 1])
        osum[c] = r2buf[c, 0] + r2buf[c, 1]
        for o in (2, 1, 3):
            for h in range(2):
                dev = (d, col(ymod(-o), z, h))
                send(osum.at[c, h, o], rbuf.at[c, o * 2 + k, 1], q_s.at[c, o, h, 1], q_r.at[c, o, k, 1], dev)
        send(osum.at[c, ok, 0], rbuf.at[c, k, 1], q_s.at[c, 0, 0, 1], q_r.at[c, 0, k, 1], sibling)
        own.append(pltpu.make_async_copy(osum.at[c, k, 0], rbuf.at[c, k, 1], ql_s.at[c, 1]))
        own[1].start()
        return own

    def tokens_back(c, own):
        for i in range(2):
            for o in range(1, NY):
                for kk in range(2):
                    landed(rbuf.at[c, o * 2 + kk, i], q_r.at[c, o, kk, i])
            landed(rbuf.at[c, ok, i], q_r.at[c, 0, ok, i])
            own[i].wait()
        got = dot(pick_t[...], rbuf[c].reshape(ALL_ROWS, CH))
        tok[c] = got.reshape(NZ, 2, T, CH)
        zs1[c, 0] = tok[c, zmod(HALF), 0].astype(BF)
        zs1[c, 1] = tok[c, zmod(-HALF), 1].astype(BF)
        send(zs1.at[c, 0], zr1.at[c, 0], t_s.at[c, 0, 0], t_r.at[c, 0, 0], up_z)
        send(zs1.at[c, 1], zr1.at[c, 1], t_s.at[c, 1, 0], t_r.at[c, 1, 0], down_z)

    def z_back(c, i):
        for w, dev in ((0, up_z), (1, down_z)):
            target = zmod(HALF - i) if w == 0 else zmod(i - HALF)
            if i == 1:
                landed(zr1.at[c, w], t_r.at[c, w, 0])
                zsn[c, w, 0, w] = (tok[c, target, w] + zr1[c, w].astype(F32)).astype(BF)
                zsn[c, w, 0, 1 - w] = tok[c, target, 1 - w].astype(BF)
            else:
                landed(zrn.at[c, w, i - 2], t_r.at[c, w, i - 1])
                zsn[c, w, i - 1] = (tok[c, target] + zrn[c, w, i - 2].astype(F32)).astype(BF)
            send(zsn.at[c, w, i - 1], zrn.at[c, w, i - 1], t_s.at[c, w, i], t_r.at[c, w, i], dev)

    def finish(c):
        for w in range(2):
            landed(zrn.at[c, w, HALF - 2], t_r.at[c, w, HALF - 1])
        total = tok[c, z] + zrn[c, 0, HALF - 2].astype(F32) + zrn[c, 1, HALF - 2].astype(F32)
        fin[c] = total.astype(BF)
        ig[c, k] = fin[c, k]
        send(fin.at[c, ok], ig.at[c, k], f_s.at[c], f_r.at[c], sibling)

    def adapters_send():
        for o in range(ND):
            flag = jnp.where(slot(xmod(o), j) == first, 1.0, 0.0)
            ad_in[o] = choose(flag, adam_in[0, 0], adam_in[0, 1]).astype(BF)
            ad_out[o] = choose(flag, adam_out[0, 0], adam_out[0, 1]).astype(BF)
            if o:
                send(ad_in.at[o], cin.at[d], a_s.at[o, 0], a_r.at[o, 0], (xmod(o), j))
                send(ad_out.at[o], cout.at[d], a_s.at[o, 1], a_r.at[o, 1], (xmod(o), j))
        cin[d] = ad_in[0]
        cout[d] = ad_out[0]

    def adapters_wait():
        for o in range(1, ND):
            landed(cin.at[xmod(-o)], a_r.at[o, 0])
            landed(cout.at[xmod(-o)], a_r.at[o, 1])

    def grads_send():
        gs_in[...] = (SCALE * dot(lgr[...], hid[...], ((0,), (0,)))).astype(BF).reshape(gs_in.shape)
        for c in range(NC):
            rows_g = xbuf[c, 1].reshape(ALL_ROWS, CC)
            r = SCALE * dot(lin[...], rows_g, ((0,), (0,)))
            gs_out[:, :, c * CC : (c + 1) * CC] = r.astype(BF).reshape(ND, R // ND, CC)
        for o in range(1, ND):
            dev = (xmod(o), j)
            send(gs_in.at[xmod(o)], gr_in.at[o], g_s.at[o, 0], g_r.at[o, 0], dev)
            send(gs_out.at[xmod(o)], gr_out.at[o], g_s.at[o, 1], g_r.at[o, 1], dev)
        gr_in[0] = gs_in[d]
        gr_out[0] = gs_out[d]

    def optimizer():
        for c in adam_loads[2:]:
            c.wait()
        for o in range(1, ND):
            landed(gr_in.at[o], g_r.at[o, 0])
            landed(gr_out.at[o], g_r.at[o, 1])
        for adam, gr, st, mo, va, ss, side in (
            (adam_in, gr_in, st_in, mo_in, va_in, ss_in, 0),
            (adam_out, gr_out, st_out, mo_out, va_out, ss_out, 1),
        ):
            for e in range(2):
                total = jnp.zeros(adam.shape[2:], F32)
                for o in range(ND):
                    flag = jnp.where(slot(xmod(-o), j) == first + e, 1.0, 0.0)
                    total = total + choose(flag, gr[o].astype(F32), jnp.zeros(adam.shape[2:], F32))
                st[e], mo[e], va[e] = adamw(adam[0, e], total, adam[1, e], adam[2, e])
            for o in range(ND):
                flag = jnp.where(slot(xmod(o), j) == first, 1.0, 0.0)
                ss[o] = choose(flag, st[0], st[1]).astype(BF)
                dst = rin if side == 0 else rout
                if o:
                    send(ss.at[o], dst.at[d], s_s.at[o, side], s_r.at[o, side], (xmod(o), j))
                else:
                    dst[d] = ss[0]

    locals_ = {}
    order = [NC] + list(range(NC))
    last = HALF + 4
    for tau in range(len(order) + last):
        for at, c in enumerate(order):
            if 0 <= tau - at <= HALF:
                z_step(c, tau - at)
        if tau == 2:
            for c in adam_loads[:2]:
                c.wait()
            adapters_send()
        if tau == HALF:
            build_pick()
        for c in range(NC):
            phase = tau - (c + 1) - HALF
            if phase == 2:
                x_forward(c)
        for c in range(NC):
            phase = tau - (c + 1) - HALF
            if phase == 1:
                y_wait(c, locals_[c])
        for c in range(NC):
            phase = tau - (c + 1) - HALF
            if phase == 0:
                locals_[c] = select(c)
        if tau == HALF + 1:
            pick_t[...] = pick[...].T
        for c in range(NC):
            phase = tau - (c + 1) - HALF
            if phase == 3:
                if c == 0:
                    for copy in loads:
                        copy.wait()
                    adapters_wait()
                x_wait(c)
                accumulate(c)
    middle()
    for tau in range(NC + HALF + 4):
        for c in range(NC):
            phase = tau - c
            if phase == 0:
                back(c)
        for c in range(NC):
            phase = tau - c
            if phase == 1:
                back_forward(c)
            elif phase == 2:
                locals_[c] = y_back(c)
            elif phase == 3:
                tokens_back(c, locals_[c])
            elif 4 <= phase < 4 + HALF - 1:
                z_back(c, phase - 3)
            elif phase == 4 + HALF - 1:
                finish(c)
        if tau == 1:
            grads_send()
        if tau == 4:
            optimizer()
    for o in range(1, ND):
        landed(rin.at[xmod(-o)], s_r.at[o, 0])
        landed(rout.at[xmod(-o)], s_r.at[o, 1])
    re_in[0] = rin[...].reshape(R, H)
    re_out[0] = rout[...].reshape(R, D)
    for c in range(NC):
        landed(ig.at[c, ok], f_r.at[c])
        for h in range(2):
            ig_out[:, c * CC + h * CH : c * CC + (h + 1) * CH] = ig[c, h]
    for c in sent:
        c.wait_send()


def per_device(
    saved_input, output_grad, route_probs, expert_choice, slot_expert, frozen_gate, frozen_up, frozen_down,
    adapter_in, adapter_out, moment_in, moment_out, second_in, second_out,
):
    T, D = saved_input.shape
    H = frozen_gate.shape[2]
    E, RD = adapter_in.shape[:2]
    R = RD * ND
    CC, CH = D // NC, D // NC // 2
    j = lax.axis_index("expert")
    meta = jnp.concatenate([expert_choice.astype(F32), route_probs], axis=1).T
    place = lax.broadcasted_iota(jnp.int32, (16, 4 * T), 1) // T == j % 4
    meta = jnp.where(place, jnp.tile(meta, (1, 4)), 0.0)
    sem = pltpu.SemaphoreType.DMA
    V = pltpu.VMEM
    scratch = [
        V((D, H), BF), V((D, H), BF), V((H, D), BF),
        V((3, E, RD, H), F32), V((3, E, RD, D), F32),
        V((NC, T, CC), BF), V((NC, NZ, 2, T, CC), BF), V((NZ, 2, 16, 4 * T), F32),
        V((ALL_ROWS, NS * T), BF), V((NS * T, ALL_ROWS), BF), V((ALL_ROWS, 128), F32),
        V((NC, 2 * NY, 2, ROWS, CC), BF), V((NC, 2, NY, ROWS, CC), BF), V((NC, 2, ND, NY, ROWS, CC), BF),
        V((ALL_ROWS, H), F32), V((ALL_ROWS, H), F32), V((ALL_ROWS, H), F32), V((ALL_ROWS, R), F32),
        V((ALL_ROWS, H), BF), V((ALL_ROWS, H), BF), V((ALL_ROWS, H), BF), V((ALL_ROWS, R), BF), V((ALL_ROWS, R), BF),
        V((NC, ND, 2, NY, ROWS, CH), BF), V((NC, 2, NY, ROWS, CH), BF), V((NC, 2, 2, NY, ROWS, CH), BF),
        V((NC, 2, NY, ROWS, CH), BF), V((NC, 2 * NY, 2, ROWS, CH), BF), V((NC, NZ, 2, T, CH), F32),
        V((NC, 2, T, CH), BF), V((NC, 2, T, CH), BF),
        V((NC, 2, HALF - 1, 2, T, CH), BF), V((NC, 2, HALF - 1, 2, T, CH), BF),
        V((NC, 2, T, CH), BF), V((NC, 2, T, CH), BF),
        V((ND, RD, H), BF), V((ND, RD, D), BF), V((ND, RD, H), BF), V((ND, RD, D), BF),
        V((ND, RD, H), BF), V((ND, RD, D), BF), V((ND, RD, H), BF), V((ND, RD, D), BF),
        V((ND, RD, H), BF), V((ND, RD, D), BF), V((ND, RD, H), BF), V((ND, RD, D), BF),
        sem((9,)), sem((NC + 1,)), sem((NC + 1,)), sem((NC + 1, 2, HALF)), sem((NC + 1, 2, HALF)),
        sem((NC, 2 * NY, 2)), sem((NC, NY, 2, 2)), sem((NC, 2)), sem((NC, 4)), sem((NC, 4)),
        sem((ND, 2)), sem((ND, 2)),
        sem((NC, 2)), sem((NC, 2)), sem((NC, 2)), sem((NC, 2)),
        sem((NC, NY, 2, 2)), sem((NC, NY, 2, 2)), sem((NC, 2)),
        sem((NC, 2, HALF)), sem((NC, 2, HALF)), sem((NC,)), sem((NC,)),
        sem((ND, 2)), sem((ND, 2)), sem((ND, 2)), sem((ND, 2)),
    ]
    vm = pl.BlockSpec(memory_space=pltpu.VMEM)
    anyspace = pl.BlockSpec(memory_space=pl.ANY)
    shape = jax.ShapeDtypeStruct
    out_shape = (
        [shape((T, D), BF)]
        + [shape((E, RD, H), F32), shape((E, RD, D), F32)] * 3
        + [shape((1, R, H), BF), shape((1, R, D), BF)]
    )
    return tuple(
        pl.pallas_call(
            kernel,
            out_shape=out_shape,
            in_specs=[vm, vm, vm, pl.BlockSpec(memory_space=pltpu.SMEM)] + [anyspace] * 9,
            out_specs=[vm] * 9,
            scratch_shapes=scratch,
            compiler_params=pltpu.CompilerParams(
                collective_id=0, has_side_effects=True, vmem_limit_bytes=62 * 1024 * 1024
            ),
            name="moe_backward",
        )(
            saved_input, output_grad, meta, slot_expert, frozen_gate, frozen_up, frozen_down,
            adapter_in, adapter_out, moment_in, moment_out, second_in, second_out,
        )
    )


def solution(mesh):
    token, state = P(("dp", "expert"), None), P("expert", "dp", None)
    slot3 = P(("dp", "expert"), None, None)
    return jax.shard_map(
        per_device,
        mesh=mesh,
        in_specs=(token,) * 4 + (P(),) + (slot3,) * 3 + (state,) * 6,
        out_specs=(token,) + (state,) * 6 + (slot3,) * 2,
        check_vma=False,
    )
```

time: 549 us -> 186 us (0.34); the launches traced: 540 us -> 185 us
  waiting for transfers between devices: 207 us -> 0 us
  Pallas kernels: 0 us -> 168 us
  local copies, waits for them, and re-layouts: 131 us -> 14.5 us
  blocking collectives: 79.6 us -> 0 us
  starting transfers between devices: 50.2 us -> 0 us
  matrix products: 33.8 us -> 0 us
  other arithmetic: 24 us -> 2 us
  between operations: 15.5 us -> 0.68 us
    all_to_all x5 -> x0, waiting for transfers between devices: 184 us -> none  [the longest x1 67.2 us: per_device(): lax.all_to_all(lax.all_to_all(send_input, 'dp', split_axis=0, concat_axis...]
    pallas_call x0 -> x1, Pallas kernels: none -> 168 us  [per_device(): pl.pallas_call(kernel, out_shape=out_shape, in_specs=[vm, vm, vm, pl.Bloc...]
    all_to_all x5 -> x0, starting transfers between devices: 50.1 us -> none  [the longest x1 19 us: per_device(): lax.all_to_all(lax.all_to_all(send_input, 'dp', split_axis=0, concat_axis...]
    all_gather x4 -> x0, blocking collectives: 43.4 us -> none  [the longest x1 11.2 us: per_device(): lax.all_gather(adapter_out.astype(jnp.bfloat16), 'dp', axis=1, tiled=True)]
    reshape x7 -> x0, local copies, waits for them, and re-layouts: 40.3 us -> none  [the longest x2 13.5 us: per_device(): back_block = back_rows.reshape(dp_count, expert_count, capacity, width)]
    gather x6 -> x0, local copies, waits for them, and re-layouts: 37.3 us -> none  [the longest x2 17.6 us: pack_rows(): send_grad = jnp.take(scaled, filler, axis=0, mode='fill', fill_value=0)]
    all_to_all x1 -> x0, blocking collectives: 36.2 us -> none  [per_device(): lax.all_to_all(back_block, 'dp', split_axis=0, concat_axis=0, tiled=True)]
    all_to_all x6 -> x0, local copies, waits for them, and re-layouts: 35.8 us -> none  [the longest x1 6.55 us: per_device(): lax.all_to_all(lax.all_to_all(send_input, 'dp', split_axis=0, concat_axis...]
  transfers between devices with their start and end apart: 7 -> 0, of which waited for: 7 -> 0; matrix products, arithmetic and copies ran while one was open for 13% -> 0% of each run, Pallas kernels for 0% -> 0%
where the time goes in v1:
time: 186 us; the launch traced here: 185 us
  Pallas kernels  168 us (90%)
  local copies, waits for them, and re-layouts  14.5 us (8%)
  other arithmetic  2 us (1%)
    pallas_call x1, Pallas kernels, per_device(): pl.pallas_call(kernel, out_shape=out_shape, in_specs=[vm, vm, vm, pl.Bloc...  168 us
    unnamed x9, local copies, waits for them, and re-layouts  14.4 us

profile of v1, /device:TPU:1, one launch (start us, length us, event | category | flops | bytes accessed | tf_op | source)
XLA Modules:
  0.0 185.4 jit_solution(6336433688039447771)
XLA Ops:
  0.7 0.7 convert_element_type.3
  1.4 0.7 maximum_bitcast_fusion
  2.1 0.1 tile.10
  2.2 0.6 fusion.meta_ref
  2.8 168.2 %moe_backward.1 = (bf16[32,2048]{1,0:T(8,128)(2,1)}, f32[2,16,768]{2,1,0:T(8,128)}, f32[2,16,2048]{2,1,0:T(8,128)}, f32[2,16,768]{2,1,0:T(8,128)}, f32[2,16,2048...) custom-call(bf16[32,2048]{1,0:T(8,128)(2,1)} %x_ref.1, ...), custom_call_target="tpu_custom_call" | custom-call | tf_op jit(solution)/shard_map/moe_backward/pallas_call | solution.py:570
  171.0 1.6 copy.32
  172.6 1.5 copy.33
  174.1 1.7 copy.34
  175.8 1.5 copy.35
  177.3 1.7 copy.36
  179.0 1.5 copy.37
  180.5 1.7 copy.38
  182.2 1.5 copy.39
  183.8 1.7 copy.40
  (3 shorter events, 0.0 us)

commit v2 on v1

--- a/solution.py
+++ b/solution.py
@@ -20,8 +20,8 @@
 ROWS = CAP * NS
 PLANE = NY * ROWS
 ALL_ROWS = ND * PLANE
+NC = 4
 HALF = NZ // 2
-NC = 4
 BF = jnp.bfloat16
 F32 = jnp.float32
 
@@ -49,9 +49,9 @@
     adam_hbm, rest = rest[:6], rest[6:]
     (ig_out, st_in, st_out, mo_in, mo_out, va_in, va_out, re_in, re_out), rest = rest[:9], rest[9:]
     (
-        wg, wu, wd, adam_in, adam_out, stage, zbuf, mbuf, pick, pick_t, weight, sendbuf, obuf, xbuf,
+        wg, wu, wd, adam_in, adam_out, stage, zbuf, mbuf, pick, pick_t, weight, sendbuf, xbuf,
         gacc, uacc, hacc, lacc, hid, ugr, ggr, lgr, lin,
-        bbuf, r1buf, r2buf, osum, rbuf, tok, zs1, zr1, zsn, zrn, fin, ig,
+        bbuf, r1buf, r2buf, osum, rbuf, zs, zr, fin, ig,
         ad_in, ad_out, cin, cout, gs_in, gs_out, gr_in, gr_out, ss_in, ss_out, rin, rout,
         hbm_sem, sib_s, sib_r, z_s, z_r, y_s, y_r, yl_s, x_s, x_r, a_s, a_r,
         b1_s, b1_r, b2_s, b2_r, q_s, q_r, ql_s, t_s, t_r, f_s, f_r, g_s, g_r, s_s, s_r,
@@ -81,8 +81,8 @@
         return lax.rem(d + o + ND, ND)
 
     sibling = (d, col(y, z, ok))
+    right, left = (xmod(1), j), (xmod(-1), j)
     up_z, down_z = (d, col(y, zmod(1), k)), (d, col(y, zmod(-1), k))
-    right, left = (xmod(1), j), (xmod(-1), j)
 
     sent = []
 
@@ -110,7 +110,7 @@
     for c in adam_loads + loads:
         c.start()
 
-    partners = [sibling, up_z, down_z]
+    partners = [sibling] + [(d, col(y, zmod(o), k)) for o in range(1, NZ)]
     partners += [(d, col(ymod(o), z, kk)) for o in range(1, NY) for kk in range(2)]
     partners += [(xmod(o), j) for o in range(1, ND)]
     barrier = pltpu.get_barrier_semaphore()
@@ -138,6 +138,8 @@
 
     def zref(c):
         return mbuf if c == NC else zbuf.at[c]
+
+    far = sorted(range(1, NZ), key=lambda o: -min(o, NZ - o))
 
     def z_send(c, i):
         buf = zref(c)
@@ -198,8 +200,8 @@
                 host = slot(d, jj)
                 other = (4 * jj + 1).astype(F32) - host
                 e = (o * 2 + kk) * 2
-                experts = jnp.where(row == e, jnp.full((NS, width), host, F32), experts)
-                experts = jnp.where(row == e + 1, jnp.full((NS, width), other, F32), experts)
+                experts = jnp.where(row == e, jnp.full((NS, width), other, F32), experts)
+                experts = jnp.where(row == e + 1, jnp.full((NS, width), host, F32), experts)
         hit = jnp.zeros((NS, width), F32)
         prob = jnp.zeros((NS, width), F32)
         for kk in range(8):
@@ -235,41 +237,30 @@
                 sendbuf[c, t] = got.astype(BF).reshape(2, ROWS, CC)
                 if o:
                     dev = (d, col(ymod(o), z, kk))
-                    send(sendbuf.at[c, t, 0], xbuf.at[c, k, 0, o], y_s.at[c, t, 0], y_r.at[c, o, k, 0], dev)
-                    send(sendbuf.at[c, t, 1], obuf.at[c, k, o], y_s.at[c, t, 1], y_r.at[c, o, k, 1], dev)
-        send(sendbuf.at[c, ok, 0], xbuf.at[c, k, 0, 0], y_s.at[c, 0, 0], y_r.at[c, 0, k, 0], sibling)
-        send(sendbuf.at[c, ok, 1], obuf.at[c, k, 0], y_s.at[c, 0, 1], y_r.at[c, 0, k, 1], sibling)
-        own = [
-            pltpu.make_async_copy(sendbuf.at[c, k, 0], xbuf.at[c, k, 0, 0], yl_s.at[c, 0]),
-            pltpu.make_async_copy(sendbuf.at[c, k, 1], obuf.at[c, k, 0], yl_s.at[c, 1]),
-        ]
-        for copy in own:
-            copy.start()
+                    send(sendbuf.at[c, t], xbuf.at[c, k, 0:2, o], y_s.at[c, t], y_r.at[c, o, k], dev)
+        send(sendbuf.at[c, ok], xbuf.at[c, k, 0:2, 0], y_s.at[c, 0], y_r.at[c, 0, k], sibling)
+        own = pltpu.make_async_copy(sendbuf.at[c, k], xbuf.at[c, k, 0:2, 0], yl_s.at[c])
+        own.start()
         return own
 
     def y_wait(c, own):
         for o in range(1, NY):
             for kk in range(2):
-                landed(obuf.at[c, kk, o], y_r.at[c, o, kk, 1])
-        landed(obuf.at[c, ok, 0], y_r.at[c, 0, ok, 1])
-        own[1].wait()
-        send(obuf.at[c], xbuf.at[c, :, 1], x_s.at[c, 0], x_r.at[c, 0], right)
-        send(obuf.at[c], xbuf.at[c, :, 3], x_s.at[c, 1], x_r.at[c, 1], left)
-        for o in range(1, NY):
-            for kk in range(2):
-                landed(xbuf.at[c, kk, 0, o], y_r.at[c, o, kk, 0])
-        landed(xbuf.at[c, ok, 0, 0], y_r.at[c, 0, ok, 0])
-        own[0].wait()
+                landed(xbuf.at[c, kk, 0:2, o], y_r.at[c, o, kk])
+        landed(xbuf.at[c, ok, 0:2, 0], y_r.at[c, 0, ok])
+        own.wait()
+        send(xbuf.at[c, :, 0], xbuf.at[c, :, 2], x_s.at[c, 0], x_r.at[c, 0], right)
+        send(xbuf.at[c, :, 0], xbuf.at[c, :, 4], x_s.at[c, 1], x_r.at[c, 1], left)
 
     def x_forward(c):
-        landed(xbuf.at[c, :, 1], x_r.at[c, 0])
-        landed(xbuf.at[c, :, 3], x_r.at[c, 1])
-        send(xbuf.at[c, 0, 1], xbuf.at[c, 0, 2], x_s.at[c, 2], x_r.at[c, 2], right)
-        send(xbuf.at[c, 1, 3], xbuf.at[c, 1, 2], x_s.at[c, 3], x_r.at[c, 3], left)
+        landed(xbuf.at[c, :, 2], x_r.at[c, 0])
+        send(xbuf.at[c, 0, 2], xbuf.at[c, 0, 3], x_s.at[c, 2], x_r.at[c, 2], right)
+        landed(xbuf.at[c, :, 4], x_r.at[c, 1])
+        send(xbuf.at[c, 1, 4], xbuf.at[c, 1, 3], x_s.at[c, 3], x_r.at[c, 3], left)
 
     def x_wait(c):
-        landed(xbuf.at[c, 0, 2], x_r.at[c, 2])
-        landed(xbuf.at[c, 1, 2], x_r.at[c, 3])
+        landed(xbuf.at[c, 0, 3], x_r.at[c, 2])
+        landed(xbuf.at[c, 1, 3], x_r.at[c, 3])
 
     NB = 256
 
@@ -288,15 +279,15 @@
 
         def body(n, carry):
             cols = pl.ds(pl.multiple_of(n * NB, NB), NB)
-            rows_x = xbuf[c, 0].reshape(ALL_ROWS, CC)
+            rows_x = xbuf[c, 0, 1:].reshape(ALL_ROWS, CC)
             add(gacc, cols, dot(rows_x, wg[c * CC : (c + 1) * CC, cols]))
             add(uacc, cols, dot(rows_x, wu[c * CC : (c + 1) * CC, cols]))
-            rows_g = xbuf[c, 1].reshape(ALL_ROWS, CC)
+            rows_g = xbuf[c, 1, 1:].reshape(ALL_ROWS, CC)
             add(hacc, cols, dot(rows_g, wd[cols, c * CC : (c + 1) * CC], ((1,), (1,))))
             return carry
 
         lax.fori_loop(0, H // NB, body, 0)
-        rows_g = xbuf[c, 1].reshape(ALL_ROWS, CC)
+        rows_g = xbuf[c, 1, 1:].reshape(ALL_ROWS, CC)
         co = cout[:, :, c * CC : (c + 1) * CC].reshape(R, CC)
         add(lacc, slice(0, R), dot(rows_g, co, ((1,), (1,))))
 
@@ -340,56 +331,40 @@
         bbuf[c, 1, 1] = bbuf[c, 1, 1] + r1buf[c, 1]
         send(bbuf.at[c, 1], r2buf.at[c, 1], b2_s.at[c, 1], b2_r.at[c, 1], left)
 
-    def y_back(c):
+    def rows_back(c, src, i):
         for o in (2, 1, 3):
             for h in range(2):
                 dev = (d, col(ymod(-o), z, h))
-                send(bbuf.at[c, 0, h, o], rbuf.at[c, o * 2 + k, 0], q_s.at[c, o, h, 0], q_r.at[c, o, k, 0], dev)
-        send(bbuf.at[c, 0, ok, 0], rbuf.at[c, k, 0], q_s.at[c, 0, 0, 0], q_r.at[c, 0, k, 0], sibling)
-        own = [pltpu.make_async_copy(bbuf.at[c, 0, k, 0], rbuf.at[c, k, 0], ql_s.at[c, 0])]
-        own[0].start()
+                send(src(h, o), rbuf.at[c, o * 2 + k, i], q_s.at[c, o, h, i], q_r.at[c, o, k, i], dev)
+        send(src(ok, 0), rbuf.at[c, k, i], q_s.at[c, 0, 0, i], q_r.at[c, 0, k, i], sibling)
+        own = pltpu.make_async_copy(src(k, 0), rbuf.at[c, k, i], ql_s.at[c, i])
+        own.start()
+        return own
+
+    def sum_back(c):
         landed(r2buf.at[c, 0], b2_r.at[c, 0])
         landed(r2buf.at[c, 1], b2_r.at[c, 1])
         osum[c] = r2buf[c, 0] + r2buf[c, 1]
-        for o in (2, 1, 3):
-            for h in range(2):
-                dev = (d, col(ymod(-o), z, h))
-                send(osum.at[c, h, o], rbuf.at[c, o * 2 + k, 1], q_s.at[c, o, h, 1], q_r.at[c, o, k, 1], dev)
-        send(osum.at[c, ok, 0], rbuf.at[c, k, 1], q_s.at[c, 0, 0, 1], q_r.at[c, 0, k, 1], sibling)
-        own.append(pltpu.make_async_copy(osum.at[c, k, 0], rbuf.at[c, k, 1], ql_s.at[c, 1]))
-        own[1].start()
-        return own
+        return rows_back(c, lambda h, o: osum.at[c, h, o], 0)
 
     def tokens_back(c, own):
-        for i in range(2):
+        for i in (1, 0):
             for o in range(1, NY):
                 for kk in range(2):
                     landed(rbuf.at[c, o * 2 + kk, i], q_r.at[c, o, kk, i])
             landed(rbuf.at[c, ok, i], q_r.at[c, 0, ok, i])
             own[i].wait()
         got = dot(pick_t[...], rbuf[c].reshape(ALL_ROWS, CH))
-        tok[c] = got.reshape(NZ, 2, T, CH)
-        zs1[c, 0] = tok[c, zmod(HALF), 0].astype(BF)
-        zs1[c, 1] = tok[c, zmod(-HALF), 1].astype(BF)
-        send(zs1.at[c, 0], zr1.at[c, 0], t_s.at[c, 0, 0], t_r.at[c, 0, 0], up_z)
-        send(zs1.at[c, 1], zr1.at[c, 1], t_s.at[c, 1, 0], t_r.at[c, 1, 0], down_z)
-
-    def z_back(c, i):
-        for w, dev in ((0, up_z), (1, down_z)):
-            target = zmod(HALF - i) if w == 0 else zmod(i - HALF)
-            if i == 1:
-                landed(zr1.at[c, w], t_r.at[c, w, 0])
-                zsn[c, w, 0, w] = (tok[c, target, w] + zr1[c, w].astype(F32)).astype(BF)
-                zsn[c, w, 0, 1 - w] = tok[c, target, 1 - w].astype(BF)
-            else:
-                landed(zrn.at[c, w, i - 2], t_r.at[c, w, i - 1])
-                zsn[c, w, i - 1] = (tok[c, target] + zrn[c, w, i - 2].astype(F32)).astype(BF)
-            send(zsn.at[c, w, i - 1], zrn.at[c, w, i - 1], t_s.at[c, w, i], t_r.at[c, w, i], dev)
+        zs[c] = got.astype(BF).reshape(NZ, 2, T, CH)
+        for o in far:
+            send(zs.at[c, zmod(o)], zr.at[c, o], t_s.at[c, o], t_r.at[c, o], (d, col(y, zmod(o), k)))
 
     def finish(c):
-        for w in range(2):
-            landed(zrn.at[c, w, HALF - 2], t_r.at[c, w, HALF - 1])
-        total = tok[c, z] + zrn[c, 0, HALF - 2].astype(F32) + zrn[c, 1, HALF - 2].astype(F32)
+        total = zs[c, z].astype(F32)
+        for o in far:
+            landed(zr.at[c, o], t_r.at[c, o])
+        for o in far:
+            total = total + zr[c, o].astype(F32)
         fin[c] = total.astype(BF)
         ig[c, k] = fin[c, k]
         send(fin.at[c, ok], ig.at[c, k], f_s.at[c], f_r.at[c], sibling)
@@ -413,7 +388,7 @@
     def grads_send():
         gs_in[...] = (SCALE * dot(lgr[...], hid[...], ((0,), (0,)))).astype(BF).reshape(gs_in.shape)
         for c in range(NC):
-            rows_g = xbuf[c, 1].reshape(ALL_ROWS, CC)
+            rows_g = xbuf[c, 1, 1:].reshape(ALL_ROWS, CC)
             r = SCALE * dot(lin[...], rows_g, ((0,), (0,)))
             gs_out[:, :, c * CC : (c + 1) * CC] = r.astype(BF).reshape(ND, R // ND, CC)
         for o in range(1, ND):
@@ -448,63 +423,58 @@
                 else:
                     dst[d] = ss[0]
 
-    locals_ = {}
-    order = [NC] + list(range(NC))
-    last = HALF + 4
-    for tau in range(len(order) + last):
-        for at, c in enumerate(order):
-            if 0 <= tau - at <= HALF:
-                z_step(c, tau - at)
-        if tau == 2:
+    owns = {}
+    early, late = {}, {}
+    for i in range(HALF + 1):
+        early.setdefault(i, []).extend([(NC, i), (0, i)])
+    for i in range(HALF + 1):
+        early.setdefault(i + 1, []).append((1, i))
+    for c in range(2, NC):
+        for i in range(HALF + 1):
+            (late if i % 2 else early).setdefault(c + 2 + i // 2, []).append((c, i))
+    for tau in range(NC + HALF + 3):
+        for c, i in early.get(tau, []):
+            z_step(c, i)
+        if tau == 1:
             for c in adam_loads[:2]:
                 c.wait()
             adapters_send()
         if tau == HALF:
             build_pick()
-        for c in range(NC):
-            phase = tau - (c + 1) - HALF
-            if phase == 2:
-                x_forward(c)
-        for c in range(NC):
-            phase = tau - (c + 1) - HALF
-            if phase == 1:
-                y_wait(c, locals_[c])
-        for c in range(NC):
-            phase = tau - (c + 1) - HALF
-            if phase == 0:
-                locals_[c] = select(c)
-        if tau == HALF + 1:
+        at = tau - HALF
+        if 0 <= at - 1 < NC:
+            y_wait(at - 1, owns[at - 1])
+        if 0 <= at - 2 < NC:
+            x_forward(at - 2)
+        if 0 <= at < NC:
+            owns[at] = select(at)
+        if at == 0:
             pick_t[...] = pick[...].T
-        for c in range(NC):
-            phase = tau - (c + 1) - HALF
-            if phase == 3:
-                if c == 0:
-                    for copy in loads:
-                        copy.wait()
-                    adapters_wait()
-                x_wait(c)
-                accumulate(c)
+        if at == 3:
+            for copy in loads:
+                copy.wait()
+            adapters_wait()
+        if 0 <= at - 3 < NC:
+            x_wait(at - 3)
+            accumulate(at - 3)
+        for c, i in late.get(tau, []):
+            z_step(c, i)
     middle()
-    for tau in range(NC + HALF + 4):
-        for c in range(NC):
-            phase = tau - c
-            if phase == 0:
-                back(c)
-        for c in range(NC):
-            phase = tau - c
-            if phase == 1:
-                back_forward(c)
-            elif phase == 2:
-                locals_[c] = y_back(c)
-            elif phase == 3:
-                tokens_back(c, locals_[c])
-            elif 4 <= phase < 4 + HALF - 1:
-                z_back(c, phase - 3)
-            elif phase == 4 + HALF - 1:
-                finish(c)
+    for tau in range(NC + 4):
+        if tau < NC:
+            back(tau)
+            owns[tau] = [None, rows_back(tau, lambda h, o, c=tau: bbuf.at[c, 0, h, o], 1)]
+        if 0 <= tau - 1 < NC:
+            back_forward(tau - 1)
+        if 0 <= tau - 2 < NC:
+            owns[tau - 2][0] = sum_back(tau - 2)
+        if 0 <= tau - 3 < NC:
+            tokens_back(tau - 3, owns[tau - 3])
+        if 0 <= tau - 4 < NC:
+            finish(tau - 4)
         if tau == 1:
             grads_send()
-        if tau == 4:
+        if tau == 5:
             optimizer()
     for o in range(1, ND):
         landed(rin.at[xmod(-o)], s_r.at[o, 0])
@@ -517,6 +487,12 @@
             ig_out[:, c * CC + h * CH : c * CC + (h + 1) * CH] = ig[c, h]
     for c in sent:
         c.wait_send()
+
+
+def hand_over(*refs):
+    n = len(refs) // 2
+    for i in range(n):
+        refs[n + i][...] = refs[i][...]
 
 
 def per_device(
@@ -539,23 +515,22 @@
         V((3, E, RD, H), F32), V((3, E, RD, D), F32),
         V((NC, T, CC), BF), V((NC, NZ, 2, T, CC), BF), V((NZ, 2, 16, 4 * T), F32),
         V((ALL_ROWS, NS * T), BF), V((NS * T, ALL_ROWS), BF), V((ALL_ROWS, 128), F32),
-        V((NC, 2 * NY, 2, ROWS, CC), BF), V((NC, 2, NY, ROWS, CC), BF), V((NC, 2, ND, NY, ROWS, CC), BF),
+        V((NC, 2 * NY, 2, ROWS, CC), BF), V((NC, 2, ND + 1, NY, ROWS, CC), BF),
         V((ALL_ROWS, H), F32), V((ALL_ROWS, H), F32), V((ALL_ROWS, H), F32), V((ALL_ROWS, R), F32),
         V((ALL_ROWS, H), BF), V((ALL_ROWS, H), BF), V((ALL_ROWS, H), BF), V((ALL_ROWS, R), BF), V((ALL_ROWS, R), BF),
         V((NC, ND, 2, NY, ROWS, CH), BF), V((NC, 2, NY, ROWS, CH), BF), V((NC, 2, 2, NY, ROWS, CH), BF),
-        V((NC, 2, NY, ROWS, CH), BF), V((NC, 2 * NY, 2, ROWS, CH), BF), V((NC, NZ, 2, T, CH), F32),
-        V((NC, 2, T, CH), BF), V((NC, 2, T, CH), BF),
-        V((NC, 2, HALF - 1, 2, T, CH), BF), V((NC, 2, HALF - 1, 2, T, CH), BF),
+        V((NC, 2, NY, ROWS, CH), BF), V((NC, 2 * NY, 2, ROWS, CH), BF),
+        V((NC, NZ, 2, T, CH), BF), V((NC, NZ, 2, T, CH), BF),
         V((NC, 2, T, CH), BF), V((NC, 2, T, CH), BF),
         V((ND, RD, H), BF), V((ND, RD, D), BF), V((ND, RD, H), BF), V((ND, RD, D), BF),
         V((ND, RD, H), BF), V((ND, RD, D), BF), V((ND, RD, H), BF), V((ND, RD, D), BF),
         V((ND, RD, H), BF), V((ND, RD, D), BF), V((ND, RD, H), BF), V((ND, RD, D), BF),
         sem((9,)), sem((NC + 1,)), sem((NC + 1,)), sem((NC + 1, 2, HALF)), sem((NC + 1, 2, HALF)),
-        sem((NC, 2 * NY, 2)), sem((NC, NY, 2, 2)), sem((NC, 2)), sem((NC, 4)), sem((NC, 4)),
+        sem((NC, 2 * NY)), sem((NC, NY, 2)), sem((NC,)), sem((NC, 4)), sem((NC, 4)),
         sem((ND, 2)), sem((ND, 2)),
         sem((NC, 2)), sem((NC, 2)), sem((NC, 2)), sem((NC, 2)),
         sem((NC, NY, 2, 2)), sem((NC, NY, 2, 2)), sem((NC, 2)),
-        sem((NC, 2, HALF)), sem((NC, 2, HALF)), sem((NC,)), sem((NC,)),
+        sem((NC, NZ)), sem((NC, NZ)), sem((NC,)), sem((NC,)),
         sem((ND, 2)), sem((ND, 2)), sem((ND, 2)), sem((ND, 2)),
     ]
     vm = pl.BlockSpec(memory_space=pltpu.VMEM)
@@ -566,21 +541,28 @@
         + [shape((E, RD, H), F32), shape((E, RD, D), F32)] * 3
         + [shape((1, R, H), BF), shape((1, R, D), BF)]
     )
+    results = pl.pallas_call(
+        kernel,
+        out_shape=out_shape,
+        in_specs=[vm, vm, vm, pl.BlockSpec(memory_space=pltpu.SMEM)] + [anyspace] * 9,
+        out_specs=[vm] * 9,
+        scratch_shapes=scratch,
+        compiler_params=pltpu.CompilerParams(
+            collective_id=0, has_side_effects=True, vmem_limit_bytes=62 * 1024 * 1024
+        ),
+        name="moe_backward",
+    )(
+        saved_input, output_grad, meta, slot_expert, frozen_gate, frozen_up, frozen_down,
+        adapter_in, adapter_out, moment_in, moment_out, second_in, second_out,
+    )
     return tuple(
         pl.pallas_call(
-            kernel,
+            hand_over,
             out_shape=out_shape,
-            in_specs=[vm, vm, vm, pl.BlockSpec(memory_space=pltpu.SMEM)] + [anyspace] * 9,
+            in_specs=[vm] * 9,
             out_specs=[vm] * 9,
-            scratch_shapes=scratch,
-            compiler_params=pltpu.CompilerParams(
-                collective_id=0, has_side_effects=True, vmem_limit_bytes=62 * 1024 * 1024
-            ),
-            name="moe_backward",
-        )(
-            saved_input, output_grad, meta, slot_expert, frozen_gate, frozen_up, frozen_down,
-            adapter_in, adapter_out, moment_in, moment_out, second_in, second_out,
-        )
+            name="hand_over",
+        )(*results)
     )
 
 

time: 186 us -> 159 us (0.85)
  local copies, waits for them, and re-layouts: 14.5 us -> 0.09 us
  Pallas kernels: 168 us -> 156 us
    pallas_call x1, Pallas kernels: 168 us -> 153 us  [per_device(): pl.pallas_call(kernel, out_shape=out_shape, in_specs=[vm, vm, vm, pl.Bloc...]
    unnamed x9 -> x0, local copies, waits for them, and re-layouts: 14.4 us -> none
    pallas_call x0 -> x1, Pallas kernels: none -> 2.57 us  [per_device(): pl.pallas_call(hand_over, out_shape=out_shape, in_specs=[vm] * 9, out_spe...]
where the time goes in v2:
time: 159 us
  Pallas kernels  156 us (98%)
  other arithmetic  2 us (1%)
    pallas_call x1, Pallas kernels, per_device(): pl.pallas_call(kernel, out_shape=out_shape, in_specs=[vm, vm, vm, pl.Bloc...  153 us

profile of v2, /device:TPU:1, one launch (start us, length us, event | category | flops | bytes accessed | tf_op | source)
XLA Modules:
  0.0 158.5 jit_solution(15562364583161564608)
XLA Ops:
  0.7 0.7 convert_element_type.3
  1.4 0.7 maximum_bitcast_fusion
  2.1 0.1 tile.10
  2.2 0.6 fusion.meta_ref
  2.8 153.2 %moe_backward.1 = (bf16[32,2048]{1,0:T(8,128)(2,1)}, f32[2,16,768]{2,1,0:T(8,128)}, f32[2,16,2048]{2,1,0:T(8,128)}, f32[2,16,768]{2,1,0:T(8,128)}, f32[2,16,2048...) custom-call(bf16[32,2048]{1,0:T(8,128)(2,1)} %x_ref.1, ...), custom_call_target="tpu_custom_call" | custom-call | tf_op jit(solution)/shard_map/moe_backward/pallas_call | solution.py:544
  155.9 2.6 %hand_over.1 = (bf16[32,2048]{1,0:T(8,128)(2,1)}, f32[2,16,768]{2,1,0:T(8,128)}, f32[2,16,2048]{2,1,0:T(8,128)}, f32[2,16,768]{2,1,0:T(8,128)}, f32[2,16,2048]{2...) custom-call(bf16[32,2048]{1,0:T(8,128)(2,1)} %get-tuple-element.18.r, ...), custom_call_target="tpu_custom_call" | custom-call | tf_op jit(solution)/shard_map/hand_over/pallas_call | solution.py:559
  (3 shorter events, 0.0 us)

commit v3 on v2

--- a/solution.py
+++ b/solution.py
@@ -442,12 +442,12 @@
         if tau == HALF:
             build_pick()
         at = tau - HALF
+        if 0 <= at < NC:
+            owns[at] = select(at)
         if 0 <= at - 1 < NC:
             y_wait(at - 1, owns[at - 1])
         if 0 <= at - 2 < NC:
             x_forward(at - 2)
-        if 0 <= at < NC:
-            owns[at] = select(at)
         if at == 0:
             pick_t[...] = pick[...].T
         if at == 3:

time: 159 us -> 159 us (level)
  no operation moved by 1% of the time
where the time goes in v3:
time: 159 us
  Pallas kernels  156 us (98%)
  other arithmetic  2 us (1%)
    pallas_call x1, Pallas kernels, per_device(): pl.pallas_call(kernel, out_shape=out_shape, in_specs=[vm, vm, vm, pl.Bloc...  154 us

profile of v3, /device:TPU:1, one launch (start us, length us, event | category | flops | bytes accessed | tf_op | source)
XLA Modules:
  0.0 159.2 jit_solution(1704830860585279708)
XLA Ops:
  0.7 0.7 convert_element_type.3
  1.4 0.7 maximum_bitcast_fusion
  2.1 0.1 tile.10
  2.2 0.6 fusion.meta_ref
  2.8 153.9 %moe_backward.1 = (bf16[32,2048]{1,0:T(8,128)(2,1)}, f32[2,16,768]{2,1,0:T(8,128)}, f32[2,16,2048]{2,1,0:T(8,128)}, f32[2,16,768]{2,1,0:T(8,128)}, f32[2,16,2048...) custom-call(bf16[32,2048]{1,0:T(8,128)(2,1)} %x_ref.1, ...), custom_call_target="tpu_custom_call" | custom-call | tf_op jit(solution)/shard_map/moe_backward/pallas_call | solution.py:544
  156.7 2.6 %hand_over.1 = (bf16[32,2048]{1,0:T(8,128)(2,1)}, f32[2,16,768]{2,1,0:T(8,128)}, f32[2,16,2048]{2,1,0:T(8,128)}, f32[2,16,768]{2,1,0:T(8,128)}, f32[2,16,2048]{2...) custom-call(bf16[32,2048]{1,0:T(8,128)(2,1)} %get-tuple-element.18.r, ...), custom_call_target="tpu_custom_call" | custom-call | tf_op jit(solution)/shard_map/hand_over/pallas_call | solution.py:559
  (3 shorter events, 0.0 us)

commit v4 on v2

--- a/solution.py
+++ b/solution.py
@@ -466,10 +466,10 @@
             owns[tau] = [None, rows_back(tau, lambda h, o, c=tau: bbuf.at[c, 0, h, o], 1)]
         if 0 <= tau - 1 < NC:
             back_forward(tau - 1)
+        if 0 <= tau - 3 < NC:
+            tokens_back(tau - 3, owns[tau - 3])
         if 0 <= tau - 2 < NC:
             owns[tau - 2][0] = sum_back(tau - 2)
-        if 0 <= tau - 3 < NC:
-            tokens_back(tau - 3, owns[tau - 3])
         if 0 <= tau - 4 < NC:
             finish(tau - 4)
         if tau == 1:

time: 159 us -> 158 us (level)
  no operation moved by 1% of the time
where the time goes in v4:
time: 158 us
  Pallas kernels  155 us (98%)
  other arithmetic  2 us (1%)
    pallas_call x1, Pallas kernels, per_device(): pl.pallas_call(kernel, out_shape=out_shape, in_specs=[vm, vm, vm, pl.Bloc...  153 us

profile of v4, /device:TPU:1, one launch (start us, length us, event | category | flops | bytes accessed | tf_op | source)
XLA Modules:
  0.0 158.2 jit_solution(15702633219749564688)
XLA Ops:
  0.7 0.7 convert_element_type.3
  1.4 0.7 maximum_bitcast_fusion
  2.1 0.1 tile.10
  2.2 0.6 fusion.meta_ref
  2.8 152.9 %moe_backward.1 = (bf16[32,2048]{1,0:T(8,128)(2,1)}, f32[2,16,768]{2,1,0:T(8,128)}, f32[2,16,2048]{2,1,0:T(8,128)}, f32[2,16,768]{2,1,0:T(8,128)}, f32[2,16,2048...) custom-call(bf16[32,2048]{1,0:T(8,128)(2,1)} %x_ref.1, ...), custom_call_target="tpu_custom_call" | custom-call | tf_op jit(solution)/shard_map/moe_backward/pallas_call | solution.py:544
  155.6 2.6 %hand_over.1 = (bf16[32,2048]{1,0:T(8,128)(2,1)}, f32[2,16,768]{2,1,0:T(8,128)}, f32[2,16,2048]{2,1,0:T(8,128)}, f32[2,16,768]{2,1,0:T(8,128)}, f32[2,16,2048]{2...) custom-call(bf16[32,2048]{1,0:T(8,128)(2,1)} %get-tuple-element.18.r, ...), custom_call_target="tpu_custom_call" | custom-call | tf_op jit(solution)/shard_map/hand_over/pallas_call | solution.py:559
  (3 shorter events, 0.0 us)
